TPU v7x, 32 devices: a whole 2x2x4 slice. The times are simulated.
32 devices in a mesh: pole: 4 (over y, x), row: 2 (over core), col: 4 (over z).
Axes of the slice: x: 2, y: 2, z: 4, core: 2. Of those that a mesh axis runs over, the one named last changes fastest.
Arguments:
- hamiltonian_panel: bfloat16 [6144, 512], P(('row', 'col'), 'pole'), may hold values from -0.005859375 to 0.005859375
- margin_panel: bfloat16 [6144, 512], P(('row', 'col'), 'pole'), may hold values from -0.0029296875 to 0.0029296875
- shifts: float32 [4, 2], P('pole'), may hold values from -2 to 2
- weights: float32 [4, 2], P('pole'), may hold values from 0.5 to 2
- pivot_inverse: float32 [4, 2, 512, 512], P('pole'), may hold values from -6 to 6
- selected_inverse: bfloat16 [4, 2, 6144, 6144], P('pole', None, 'row', 'col'), may hold values from -6 to 6
Outputs:
- inverse_column: float32 [4, 6144, 2, 512], P('pole', ('row', 'col'))
- inverse_pivot: float32 [4, 2, 512, 512], P('pole')
- density_column: float32 [6144, 512], P(('row', 'col'), 'pole')
- density_pivot: float32 [512, 512], P('pole')
All inputs are finite; a program needn't handle non-finite values.
Results may differ from a plain program's by a relative error of at most 0.0037.
Values may be sent and summed in bfloat16 or wider, within the bound.
A program may use at most 128 MiB of HBM per device.

v0:
```python
import jax
import jax.numpy as jnp
from jax import lax
from jax.sharding import PartitionSpec as P

HALVES = 2


def precise(left, right):
    return jnp.dot(left, right, precision=lax.Precision.HIGH, preferred_element_type=jnp.float32)


def gather_panel(pair):
    rows = pair.shape[0] // 2
    return (
        lax.all_gather(pair[:rows], "pole", axis=1, tiled=True),
        lax.all_gather(pair[rows:], "pole", axis=1, tiled=True),
    )


def exchange_sum(pieces, axis):
    return jnp.sum(lax.all_to_all(pieces, axis, 0, 0, tiled=True).astype(jnp.float32), axis=0)


def factor_panel(pair, shift, inverse):
    hamiltonian_f = pair[0].astype(jnp.float32)
    margin_f = pair[1].astype(jnp.float32)
    real_part = hamiltonian_f - shift[0] * margin_f
    imag_part = -shift[1] * margin_f
    lower_real = precise(real_part, inverse[0]) - precise(imag_part, inverse[1])
    lower_imag = precise(real_part, inverse[1]) + precise(imag_part, inverse[0])
    return (lower_real.astype(jnp.bfloat16), lower_imag.astype(jnp.bfloat16))


def half_dot(left, right):
    return lax.dot_general(
        left, right, (((0,), (0,)), ((), ())), preferred_element_type=jnp.float32
    )


def body(hamiltonian_panel, margin_panel, shifts, weights, pivot_inverse, selected_inverse):
    shift = shifts[0]
    weight = weights[0]
    inverse = pivot_inverse[0]
    block_real = selected_inverse[0, 0]
    block_imag = selected_inverse[0, 1]
    n_row = lax.axis_size("row")
    n_col = lax.axis_size("col")
    n_pole = lax.axis_size("pole")
    width = inverse.shape[-1]
    part = width // HALVES
    own_pair = jnp.concatenate([hamiltonian_panel, margin_panel], axis=0)
    order = [(n_row * c + r, r * n_col + c) for r in range(n_row) for c in range(n_col)]
    met_pair = gather_panel(lax.ppermute(own_pair, ("row", "col"), order))
    met_real, met_imag = factor_panel(met_pair, shift, inverse)
    partials = []
    for h in range(HALVES):
        cut = slice(h * part, (h + 1) * part)
        mine = jnp.concatenate([met_real[:, cut], met_imag[:, cut]], axis=1)
        rows = lax.all_gather(mine, "row", axis=0, tiled=True)
        turned = jnp.concatenate([rows[:, part:], -rows[:, :part]], axis=1)
        total = jnp.dot(block_imag, turned, preferred_element_type=jnp.float32) - jnp.dot(
            block_real, rows, preferred_element_type=jnp.float32
        )
        partials.append(total.astype(jnp.bfloat16))
    own_pair, partials[-1] = lax.optimization_barrier((own_pair, partials[-1]))
    own_real, own_imag = factor_panel(gather_panel(own_pair), shift, inverse)
    lower = jnp.concatenate([own_real, own_imag], axis=1)
    columns = []
    updates = []
    for h in range(HALVES):
        column = exchange_sum(partials[h].reshape(n_col, -1, 2 * part), "col")
        high = column.astype(jnp.bfloat16)
        low = (column - high.astype(jnp.float32)).astype(jnp.bfloat16)
        square = half_dot(lower, high) + half_dot(lower, low)
        update = jnp.stack(
            [
                square[:width, :part] - square[width:, part:],
                square[:width, part:] + square[width:, :part],
            ]
        )
        updates.append(update)
        columns.append(column.reshape(column.shape[0], 2, part))
    column = jnp.concatenate(columns, axis=2)
    update = jnp.concatenate(updates, axis=2)
    pieces = update.reshape(n_row * n_col, -1, width).astype(jnp.bfloat16)
    piece = lax.optimization_barrier(exchange_sum(pieces, ("row", "col")))
    update = lax.all_gather(piece.astype(jnp.bfloat16), ("row", "col"), axis=0, tiled=True)
    pivot = inverse - update.reshape(2, width, width).astype(jnp.float32)
    column_density = weight[0] * column[:, 0] - weight[1] * column[:, 1]
    share = width // n_pole
    column_share = exchange_sum(column_density.reshape(-1, n_pole, share).swapaxes(0, 1), "pole")
    pivot_density = weight[0] * pivot[0] - weight[1] * pivot[1]
    pivot_share = exchange_sum(pivot_density.reshape(n_pole, share, width), "pole")
    return (column[None], pivot[None], column_share, pivot_share)


def solution(mesh):
    return jax.shard_map(
        body,
        mesh=mesh,
        in_specs=(
            P(("row", "col"), "pole"),
            P(("row", "col"), "pole"),
            P("pole", None),
            P("pole", None),
            P("pole", None, None, None),
            P("pole", None, "row", "col"),
        ),
        out_specs=(
            P("pole", ("row", "col"), None, None),
            P("pole", None, None, None),
            P(("row", "col"), "pole"),
            P("pole", None),
        ),
        check_vma=False,
    )
```

profile of v0, /device:TPU:0, one launch (start us, length us, event | category | flops | bytes accessed | tf_op | source)
XLA Modules:
  0.0 332.2 jit_solution(18348677781217761953)
XLA Ops:
  7.2 1.1 constant_dynamic-update-slice_fusion.1
  10.0 1.3 fusion.91
  12.0 12.6 %all_gather.22 = bf16[768,512]{1,0:T(8,128)(2,1)S(1)} all-gather(bf16[768,128]{1,0:T(8,128)(2,1)S(1)} %get-tuple-element.27), channel_id=1, replica_groups=mesh['pole'=4,'row'=2,'col'=4] {'pole'}, dimensions={1}, use_global_device_ids=true | all-gather | bytes 983040 | tf_op jit(solution)/shard_map/all_gather | solution.py:17
  24.5 1.6 fusion.21
  26.2 1.6 fusion.20
  27.8 12.2 %all_gather.21 = bf16[768,512]{1,0:T(8,128)(2,1)S(1)} all-gather(bf16[768,128]{1,0:T(8,128)(2,1)S(1)} %get-tuple-element.26), channel_id=1, replica_groups=mesh['pole'=4,'row'=2,'col'=4] {'pole'}, dimensions={1}, use_global_device_ids=true | all-gather | bytes 983040 | tf_op jit(solution)/shard_map/all_gather | solution.py:16
  40.0 2.3 subtract_convert_fusion.5
  42.3 2.3 add_convert_fusion.1
  45.7 19.8 %all-gather.6.cloned.1.call-done = bf16[1536,512]{0,1:T(8,128)(2,1)} async-done(((bf16[768,512]{0,1:T(8,128)(2,1)}), bf16[1536,512]{0,1:T(8,128)(2,1)}) %all-gather.6.cloned.1.call-update) | async-done | bytes 1572880 | tf_op jit(solution)/shard_map/all_gather | solution.py:60
  65.5 1.6 fusion.85
  67.4 7.7 %fusion = f32[512,3072]{1,0:T(8,128)S(1)} fusion(bf16[1536,512]{0,1:T(8,128)(2,1)S(1)} %copy-done.6, bf16[1,2,3072,1536]{3,2,1,0:T(8,128)(2,1)} %param.11), kind=kOutput, calls=%fused_computation | convolution fusion | flops 4831838208 | bytes 17301504 | tf_op jit(solution)/shard_map/dot_general | solution.py:62
  75.1 7.6 %fusion.16 = bf16[3072,512]{0,1:T(8,128)(2,1)S(1)} fusion(f32[512,3072]{1,0:T(8,128)S(1)} %fusion, bf16[1,2,3072,1536]{3,2,1,0:T(8,128)(2,1)} %param.11, bf16[1536,256]{0,1:T(8,128)(2,1)S(1)} %get-tuple-element.19, bf16[1536,256]{0,1:T(8,128)(2,1)S(1)} %get-tuple-element.18), kind=kOutput, calls=%fused_computation.21 | convolution fusion | flops 4838129664 | bytes 20447232 | tf_op jit(solution)/shard_map/dot_general | solution.py:62
  82.7 1.9 copy.31
  84.6 4.9 %all-to-all-start.1 = ((bf16[4,768,512]{1,2,0:T(8,128)(2,1)}), bf16[4,768,512]{1,2,0:T(8,128)(2,1)}, u32[]{:S(2)}, u32[]{:S(2)}) async-start(bf16[4,768,512]{1,2,0:T(8,128)(2,1)} %bitcast.79), calls=%async_computation.1 | async-start | bytes 6291456 | tf_op jit(solution)/shard_map/all_to_all | solution.py:22
  90.4 13.2 %all-gather.4.cloned.1.call-done = bf16[1536,512]{0,1:T(8,128)(2,1)} async-done(((bf16[768,512]{0,1:T(8,128)(2,1)}), bf16[1536,512]{0,1:T(8,128)(2,1)}) %all-gather.4.cloned.1.call-update) | async-done | bytes 1572880 | tf_op jit(solution)/shard_map/all_gather | solution.py:60
  103.7 1.6 fusion.84
  105.5 7.7 %fusion.2 = f32[512,3072]{1,0:T(8,128)S(1)} fusion(bf16[1536,512]{0,1:T(8,128)(2,1)S(1)} %copy-done.7, bf16[1,2,3072,1536]{3,2,1,0:T(8,128)(2,1)} %param.11), kind=kOutput, calls=%fused_computation.2 | convolution fusion | flops 4831838208 | bytes 17301504 | tf_op jit(solution)/shard_map/dot_general | solution.py:62
  113.2 7.6 %subtract_convert_fusion.1 = bf16[512,3072]{1,0:T(8,128)(2,1)S(1)} fusion(f32[512,3072]{1,0:T(8,128)S(1)} %fusion.2, bf16[1,2,3072,1536]{3,2,1,0:T(8,128)(2,1)} %param.11, bf16[1536,256]{0,1:T(8,128)(2,1)S(1)} %get-tuple-element.17, bf16[1536,256]{0,1:T(8,128)(2,1)S(1)} %get-tuple-element.16), kind=kOutput, calls=%fused_computation.15 | convolution fusion | flops 4838129664 | bytes 20447232 | tf_op jit(solution)/shard_map/dot_general | solution.py:62
  120.9 1.9 copy.32
  122.8 38.0 %all-to-all-done.1 = bf16[4,768,512]{1,2,0:T(8,128)(2,1)} async-done(((bf16[4,768,512]{1,2,0:T(8,128)(2,1)}), bf16[4,768,512]{1,2,0:T(8,128)(2,1)}, u32[]{:S(2)}, u32[]{:S(2)}) %all-to-all-start.1) | async-done | bytes 3145760 | tf_op jit(solution)/shard_map/all_to_all | solution.py:22
  160.8 4.7 %all-to-all-start = ((bf16[4,768,512]{1,2,0:T(8,128)(2,1)}), bf16[4,768,512]{1,2,0:T(8,128)(2,1)}, u32[]{:S(2)}, u32[]{:S(2)}) async-start(bf16[4,768,512]{1,2,0:T(8,128)(2,1)} %bitcast.78), calls=%async_computation | async-start | bytes 6291456 | tf_op jit(solution)/shard_map/all_to_all | solution.py:22
  165.5 11.4 %all_gather.26 = bf16[768,512]{1,0:T(8,128)(2,1)S(1)} all-gather(bf16[768,128]{1,0:T(8,128)(2,1)S(1)} %get-tuple-element.25), channel_id=1, replica_groups=mesh['pole'=4,'row'=2,'col'=4] {'pole'}, dimensions={1}, use_global_device_ids=true | all-gather | bytes 983040 | tf_op jit(solution)/shard_map/all_gather | solution.py:17
  176.9 12.1 %all_gather.25 = bf16[768,512]{1,0:T(8,128)(2,1)S(1)} all-gather(bf16[768,128]{1,0:T(8,128)(2,1)S(1)} %get-tuple-element.24), channel_id=1, replica_groups=mesh['pole'=4,'row'=2,'col'=4] {'pole'}, dimensions={1}, use_global_device_ids=true | all-gather | bytes 983040 | tf_op jit(solution)/shard_map/all_gather | solution.py:16
  189.0 2.3 fusion.37
  191.3 2.3 fusion.39
  193.6 1.6 add_convert_fusion
  195.2 1.6 subtract_convert_fusion.4
  196.9 2.7 convert_reduce_fusion
  199.6 1.0 fusion.73
  200.7 1.0 convolution_add_fusion
  202.6 33.2 %all-to-all-done = bf16[4,768,512]{1,2,0:T(8,128)(2,1)} async-done(((bf16[4,768,512]{1,2,0:T(8,128)(2,1)}), bf16[4,768,512]{1,2,0:T(8,128)(2,1)}, u32[]{:S(2)}, u32[]{:S(2)}) %all-to-all-start) | async-done | bytes 3145760 | tf_op jit(solution)/shard_map/all_to_all | solution.py:22
  235.9 2.6 convert_reduce_fusion.1
  238.4 1.0 fusion.76
  239.6 1.0 convolution_add_fusion.1
  241.7 1.3 copy.22
  243.0 29.8 %all_to_all.25 = bf16[8,128,512]{2,1,0:T(8,128)(2,1)S(1)} all-to-all(bf16[8,128,512]{2,1,0:T(8,128)(2,1)} %bitcast.81), channel_id=1, replica_groups=mesh['pole'=4,'row'=2,'col'=4] {'row','col'}, dimensions={0} | all-to-all | bytes 2097152 | tf_op jit(solution)/shard_map/all_to_all | solution.py:22
  274.2 4.4 %fusion.28 = f32[768,1,512]{0,2,1:T(8,128)} fusion(f32[768,2,256]{0,2,1:T(8,128)} %bitcast.74, f32[768,2,256]{0,2,1:T(8,128)} %bitcast.72, f32[]{:T(128)} %bitcast.18, f32[]{:T(128)} %bitcast.17), kind=kLoop, calls=%fused_computation.41 | loop fusion | flops 1966080 | bytes 4718600 | tf_op jit(solution)/shard_map/sub | solution.py:90
  278.7 3.1 copy.23
  281.8 4.4 %all-to-all-start.3 = ((f32[4,768,128]{2,1,0:T(8,128)}), f32[4,768,128]{2,1,0:T(8,128)}, u32[]{:S(2)}, u32[]{:S(2)}) async-start(f32[4,768,128]{2,1,0:T(8,128)} %copy.23), calls=%async_computation.3 | async-start | bytes 3145728 | tf_op jit(solution)/shard_map/all_to_all | solution.py:22
  286.1 8.5 %all-gather.8.cloned.1.call-done = bf16[1024,512]{1,0:T(8,128)(2,1)} async-done(((bf16[128,512]{1,0:T(8,128)(2,1)}), bf16[1024,512]{1,0:T(8,128)(2,1)}) %all-gather.8.cloned.1.call-update) | async-done | bytes 1048592 | tf_op jit(solution)/shard_map/all_gather | solution.py:88
  294.6 1.5 convert_element_type.115
  297.5 2.5 fusion.43
  300.0 6.3 %all-to-all-done.3 = f32[4,768,128]{2,1,0:T(8,128)} async-done(((f32[4,768,128]{2,1,0:T(8,128)}), f32[4,768,128]{2,1,0:T(8,128)}, u32[]{:S(2)}, u32[]{:S(2)}) %all-to-all-start.3) | async-done | bytes 1572896 | tf_op jit(solution)/shard_map/all_to_all | solution.py:22
  306.2 3.5 %all-to-all-start.4 = ((f32[4,128,512]{2,1,0:T(8,128)}), f32[4,128,512]{2,1,0:T(8,128)S(1)}, u32[]{:S(2)}, u32[]{:S(2)}) async-start(f32[4,128,512]{2,1,0:T(8,128)} %bitcast.23), calls=%async_computation.4 | async-start | bytes 2097152 | tf_op jit(solution)/shard_map/all_to_all | solution.py:22
  309.8 3.7 %fusion.19 = f32[1,768,2,512]{1,3,2,0:T(8,128)} fusion(f32[768,2,256]{0,2,1:T(8,128)} %bitcast.73, f32[768,2,256]{0,2,1:T(8,128)} %bitcast.75), kind=kLoop, calls=%fused_computation.22 | loop fusion | flops 786432 | bytes 6291456 | tf_op jit(solution)/shard_map/broadcast_in_dim | solution.py:95
  313.5 5.7 %copy.24 = f32[1,768,2,512]{3,2,1,0:T(2,128)} copy(f32[1,768,2,512]{1,3,2,0:T(8,128)} %fusion.19) | data formatting | bytes 6291456
  319.2 2.3 reduce_sum.48
  321.5 3.4 %sub.62 = f32[1,2,512,512]{3,2,1,0:T(8,128)} subtract(f32[1,2,512,512]{3,2,1,0:T(8,128)S(1)} %copy-done, f32[1,2,512,512]{3,2,1,0:T(8,128)} %bitcast.77) | non-fusion elementwise | flops 524288 | bytes 6291456 | tf_op jit(solution)/shard_map/sub | solution.py:89
  (42 shorter events, 10.0 us)
Async XLA Ops:
  7.2 17.4 %copy-start = (f32[1,2,512,512]{3,2,1,0:T(8,128)S(1)}, f32[1,2,512,512]{3,2,1,0:T(8,128)}, u32[]{:S(2)}) copy-start(f32[1,2,512,512]{3,2,1,0:T(8,128)} %param.10) | copy-start | bytes 6291460
  7.2 58.3 %all-gather.6.cloned.1.call-start = ((), (), s32[]{:S(2)}) async-start(), calls=%async_computation.6 | async-start | bytes 2359296 | tf_op jit(solution)/shard_map/all_gather | solution.py:60
  9.3 2.7 collective-permute-start
  65.5 1.9 copy-start.6
  84.6 76.2 %all-to-all-start.1 = ((bf16[4,768,512]{1,2,0:T(8,128)(2,1)}), bf16[4,768,512]{1,2,0:T(8,128)(2,1)}, u32[]{:S(2)}, u32[]{:S(2)}) async-start(bf16[4,768,512]{1,2,0:T(8,128)(2,1)} %bitcast.79), calls=%async_computation.1 | async-start | bytes 6291456 | tf_op jit(solution)/shard_map/all_to_all | solution.py:22
  89.4 14.2 %all-gather.4.cloned.1.call-start = ((), (), s32[]{:S(2)}) async-start(), calls=%async_computation.5 | async-start | bytes 2359296 | tf_op jit(solution)/shard_map/all_gather | solution.py:60
  103.7 1.9 copy-start.7
  160.8 75.1 %all-to-all-start = ((bf16[4,768,512]{1,2,0:T(8,128)(2,1)}), bf16[4,768,512]{1,2,0:T(8,128)(2,1)}, u32[]{:S(2)}, u32[]{:S(2)}) async-start(bf16[4,768,512]{1,2,0:T(8,128)(2,1)} %bitcast.78), calls=%async_computation | async-start | bytes 6291456 | tf_op jit(solution)/shard_map/all_to_all | solution.py:22
  165.4 129.2 %all-gather.8.cloned.1.call-start = ((), (), s32[]{:S(2)}) async-start(), calls=%async_computation.7 | async-start | bytes 1179648 | tf_op jit(solution)/shard_map/all_gather | solution.py:88
  196.9 3.7 %copy-start.3 = (bf16[768,512]{0,1:T(8,128)(2,1)}, bf16[768,512]{0,1:T(8,128)(2,1)S(1)}, u32[]{:S(2)}) copy-start(bf16[768,512]{0,1:T(8,128)(2,1)S(1)} %subtract_convert_fusion.4) | copy-start | bytes 2359300
  199.6 1.1 copy-start.1
  235.9 2.6 copy-start.4
  238.4 1.2 copy-start.2
  240.6 1.0 copy-start.8
  243.0 30.6 %copy-start.9 = (f32[1,2]{1,0:T(1,128)S(1)}, f32[1,2]{1,0:T(1,128)}, u32[]{:S(2)}) copy-start(f32[1,2]{1,0:T(1,128)} %param.9) | copy-start | bytes 28
  281.8 24.5 %all-to-all-start.3 = ((f32[4,768,128]{2,1,0:T(8,128)}), f32[4,768,128]{2,1,0:T(8,128)}, u32[]{:S(2)}, u32[]{:S(2)}) async-start(f32[4,768,128]{2,1,0:T(8,128)} %copy.23), calls=%async_computation.3 | async-start | bytes 3145728 | tf_op jit(solution)/shard_map/all_to_all | solution.py:22
  296.2 1.3 copy-start.5
  306.2 18.7 %all-to-all-start.4 = ((f32[4,128,512]{2,1,0:T(8,128)}), f32[4,128,512]{2,1,0:T(8,128)S(1)}, u32[]{:S(2)}, u32[]{:S(2)}) async-start(f32[4,128,512]{2,1,0:T(8,128)} %bitcast.23), calls=%async_computation.4 | async-start | bytes 2097152 | tf_op jit(solution)/shard_map/all_to_all | solution.py:22
Sparse Core Ops, SparseCore 0:
  45.8 19.6 all-gather.5
  92.4 11.2 all-gather.3
  273.7 20.8 all-gather.7
where the time goes:
time: 333 us; the launch traced here: 332 us
  waiting for transfers between devices  119 us (36%)
  blocking collectives  78.1 us (23%)
  matrix products  50.3 us (15%)
  other arithmetic  31.3 us (9%)
  local copies, waits for them, and re-layouts  20.5 us (6%)
  starting transfers between devices  18.2 us (5%)
  between operations  14.7 us (4%)
    all_to_all x4, waiting for transfers between devices, exchange_sum(): lax.all_to_all(pieces, axis, 0, 0, tiled=True).astype(jnp.float32)  77.5 us
    all_gather x2, waiting for transfers between devices, body(): rows = lax.all_gather(mine, 'row', axis=0, tiled=True)  33.1 us
    all_to_all x1, blocking collectives, exchange_sum(): lax.all_to_all(pieces, axis, 0, 0, tiled=True).astype(jnp.float32)  29.8 us
    all_gather x2, blocking collectives, gather_panel(): lax.all_gather(pair[:rows], 'pole', axis=1, tiled=True)  24.3 us
    all_gather x2, blocking collectives, gather_panel(): lax.all_gather(pair[rows:], 'pole', axis=1, tiled=True)  24 us
    all_to_all x4, starting transfers between devices, exchange_sum(): lax.all_to_all(pieces, axis, 0, 0, tiled=True).astype(jnp.float32)  17.4 us
    dot_general x8, matrix products, precise(): jnp.dot(left, right, precision=lax.Precision.HIGH, preferred_element_type...  15.6 us
    dot_general x2, matrix products, body(): jnp.dot(block_real, rows, preferred_element_type=jnp.float32)  15.3 us
  transfers between devices with their start and end apart: 8, of which 6 were waited for; matrix products, arithmetic and copies ran while one was open for 19% of the time, Pallas kernels for 0%

commit v1 on v0

--- a/solution.py
+++ b/solution.py
@@ -4,6 +4,19 @@
 from jax.sharding import PartitionSpec as P
 
 HALVES = 2
+
+
+def ring_gather(x, axis, dim):
+    ways = lax.axis_size(axis)
+    up = [(d, (d + 1) % ways) for d in range(ways)]
+    down = [(d, (d - 1) % ways) for d in range(ways)]
+    earlier, later = ([x], [x])
+    for _ in range(ways // 2):
+        earlier.append(lax.ppermute(earlier[-1], axis, up))
+    for _ in range((ways - 1) // 2):
+        later.append(lax.ppermute(later[-1], axis, down))
+    line = jnp.concatenate([*earlier[::-1], *later[1:]], axis=dim)
+    return jnp.roll(line, (lax.axis_index(axis) - ways // 2) * x.shape[dim], axis=dim)
 
 
 def precise(left, right):
@@ -85,7 +98,7 @@
     update = jnp.concatenate(updates, axis=2)
     pieces = update.reshape(n_row * n_col, -1, width).astype(jnp.bfloat16)
     piece = lax.optimization_barrier(exchange_sum(pieces, ("row", "col")))
-    update = lax.all_gather(piece.astype(jnp.bfloat16), ("row", "col"), axis=0, tiled=True)
+    update = ring_gather(piece.astype(jnp.bfloat16), ("row", "col"), 0)
     pivot = inverse - update.reshape(2, width, width).astype(jnp.float32)
     column_density = weight[0] * column[:, 0] - weight[1] * column[:, 1]
     share = width // n_pole

time: 333 us -> 355 us (1.066)
  waiting for transfers between devices: 119 us -> 131 us
  starting transfers between devices: 18.2 us -> 28.6 us
    ppermute x0 -> x7, waiting for transfers between devices: none -> 18.3 us  [the longest x4 14.3 us: ring_gather(): earlier.append(lax.ppermute(earlier[-1], axis, up))]
    ppermute x0 -> x7, starting transfers between devices: none -> 10.5 us  [the longest x3 10.4 us: ring_gather(): later.append(lax.ppermute(later[-1], axis, down))]
    all_gather x1 -> x0, waiting for transfers between devices: 8.52 us -> none  [body(): lax.all_gather(piece.astype(jnp.bfloat16), ('row', 'col'), axis=0, tiled=...]
    unnamed x22 -> x37, local copies, waits for them, and re-layouts: 9.24 us -> 9.45 us
  transfers between devices with their start and end apart: 8 -> 14, of which waited for: 6 -> 10; matrix products, arithmetic and copies ran while one was open for 19% -> 17% of each run, Pallas kernels for 0% -> 0%
where the time goes in v1:
time: 355 us; the launch traced here: 354 us
  waiting for transfers between devices  131 us (37%)
  blocking collectives  78.1 us (22%)
  matrix products  50.3 us (14%)
  other arithmetic  29.4 us (8%)
  starting transfers between devices  28.6 us (8%)
  local copies, waits for them, and re-layouts  20.7 us (6%)
  between operations  15.1 us (4%)
    all_to_all x4, waiting for transfers between devices, exchange_sum(): lax.all_to_all(pieces, axis, 0, 0, tiled=True).astype(jnp.float32)  80.1 us
    all_gather x2, waiting for transfers between devices, body(): rows = lax.all_gather(mine, 'row', axis=0, tiled=True)  33.1 us
    all_to_all x1, blocking collectives, exchange_sum(): lax.all_to_all(pieces, axis, 0, 0, tiled=True).astype(jnp.float32)  29.8 us
    all_gather x2, blocking collectives, gather_panel(): lax.all_gather(pair[:rows], 'pole', axis=1, tiled=True)  24.3 us
    all_gather x2, blocking collectives, gather_panel(): lax.all_gather(pair[rows:], 'pole', axis=1, tiled=True)  24 us
    all_to_all x4, starting transfers between devices, exchange_sum(): lax.all_to_all(pieces, axis, 0, 0, tiled=True).astype(jnp.float32)  17.4 us
    dot_general x8, matrix products, precise(): jnp.dot(left, right, precision=lax.Precision.HIGH, preferred_element_type...  15.6 us
    dot_general x2, matrix products, body(): jnp.dot(block_real, rows, preferred_element_type=jnp.float32)  15.3 us
  transfers between devices with their start and end apart: 14, of which 10 were waited for; matrix products, arithmetic and copies ran while one was open for 17% of the time, Pallas kernels for 0%

profile of v1, /device:TPU:0, one launch (start us, length us, event | category | flops | bytes accessed | tf_op | source)
XLA Modules:
  0.0 353.7 jit_solution(4067947522591740570)
XLA Ops:
  10.0 1.3 fusion.91
  12.0 12.6 %all_gather.19 = bf16[768,512]{1,0:T(8,128)(2,1)S(1)} all-gather(bf16[768,128]{1,0:T(8,128)(2,1)S(1)} %get-tuple-element.27), channel_id=1, replica_groups=mesh['pole'=4,'row'=2,'col'=4] {'pole'}, dimensions={1}, use_global_device_ids=true | all-gather | bytes 983040 | tf_op jit(solution)/shard_map/all_gather | solution.py:30
  24.5 1.6 fusion.21
  26.2 1.6 fusion.20
  27.8 12.2 %all_gather.18 = bf16[768,512]{1,0:T(8,128)(2,1)S(1)} all-gather(bf16[768,128]{1,0:T(8,128)(2,1)S(1)} %get-tuple-element.26), channel_id=1, replica_groups=mesh['pole'=4,'row'=2,'col'=4] {'pole'}, dimensions={1}, use_global_device_ids=true | all-gather | bytes 983040 | tf_op jit(solution)/shard_map/all_gather | solution.py:29
  40.0 2.3 subtract_convert_fusion.5
  42.3 2.3 add_convert_fusion.1
  45.7 19.8 %all-gather.5.cloned.1.call-done = bf16[1536,512]{0,1:T(8,128)(2,1)} async-done(((bf16[768,512]{0,1:T(8,128)(2,1)}), bf16[1536,512]{0,1:T(8,128)(2,1)}) %all-gather.5.cloned.1.call-update) | async-done | bytes 1572880 | tf_op jit(solution)/shard_map/all_gather | solution.py:73
  65.5 1.6 fusion.85
  67.4 7.7 %fusion = f32[512,3072]{1,0:T(8,128)S(1)} fusion(bf16[1536,512]{0,1:T(8,128)(2,1)S(1)} %copy-done.6, bf16[1,2,3072,1536]{3,2,1,0:T(8,128)(2,1)} %param.11), kind=kOutput, calls=%fused_computation | convolution fusion | flops 4831838208 | bytes 17301504 | tf_op jit(solution)/shard_map/dot_general | solution.py:75
  75.1 7.6 %fusion.16 = bf16[3072,512]{0,1:T(8,128)(2,1)S(1)} fusion(f32[512,3072]{1,0:T(8,128)S(1)} %fusion, bf16[1,2,3072,1536]{3,2,1,0:T(8,128)(2,1)} %param.11, bf16[1536,256]{0,1:T(8,128)(2,1)S(1)} %get-tuple-element.19, bf16[1536,256]{0,1:T(8,128)(2,1)S(1)} %get-tuple-element.18), kind=kOutput, calls=%fused_computation.21 | convolution fusion | flops 4838129664 | bytes 20447232 | tf_op jit(solution)/shard_map/dot_general | solution.py:75
  82.7 1.9 copy.31
  84.6 4.9 %all-to-all-start.1 = ((bf16[4,768,512]{1,2,0:T(8,128)(2,1)}), bf16[4,768,512]{1,2,0:T(8,128)(2,1)}, u32[]{:S(2)}, u32[]{:S(2)}) async-start(bf16[4,768,512]{1,2,0:T(8,128)(2,1)} %bitcast.79), calls=%async_computation.1 | async-start | bytes 6291456 | tf_op jit(solution)/shard_map/all_to_all | solution.py:35
  90.4 13.2 %all-gather.3.cloned.1.call-done = bf16[1536,512]{0,1:T(8,128)(2,1)} async-done(((bf16[768,512]{0,1:T(8,128)(2,1)}), bf16[1536,512]{0,1:T(8,128)(2,1)}) %all-gather.3.cloned.1.call-update) | async-done | bytes 1572880 | tf_op jit(solution)/shard_map/all_gather | solution.py:73
  103.7 1.6 fusion.84
  105.5 7.7 %fusion.2 = f32[512,3072]{1,0:T(8,128)S(1)} fusion(bf16[1536,512]{0,1:T(8,128)(2,1)S(1)} %copy-done.7, bf16[1,2,3072,1536]{3,2,1,0:T(8,128)(2,1)} %param.11), kind=kOutput, calls=%fused_computation.2 | convolution fusion | flops 4831838208 | bytes 17301504 | tf_op jit(solution)/shard_map/dot_general | solution.py:75
  113.2 7.6 %subtract_convert_fusion.1 = bf16[512,3072]{1,0:T(8,128)(2,1)S(1)} fusion(f32[512,3072]{1,0:T(8,128)S(1)} %fusion.2, bf16[1,2,3072,1536]{3,2,1,0:T(8,128)(2,1)} %param.11, bf16[1536,256]{0,1:T(8,128)(2,1)S(1)} %get-tuple-element.17, bf16[1536,256]{0,1:T(8,128)(2,1)S(1)} %get-tuple-element.16), kind=kOutput, calls=%fused_computation.15 | convolution fusion | flops 4838129664 | bytes 20447232 | tf_op jit(solution)/shard_map/dot_general | solution.py:75
  120.9 1.9 copy.32
  122.8 38.0 %all-to-all-done.1 = bf16[4,768,512]{1,2,0:T(8,128)(2,1)} async-done(((bf16[4,768,512]{1,2,0:T(8,128)(2,1)}), bf16[4,768,512]{1,2,0:T(8,128)(2,1)}, u32[]{:S(2)}, u32[]{:S(2)}) %all-to-all-start.1) | async-done | bytes 3145760 | tf_op jit(solution)/shard_map/all_to_all | solution.py:35
  160.8 4.6 %all-to-all-start = ((bf16[4,768,512]{1,2,0:T(8,128)(2,1)}), bf16[4,768,512]{1,2,0:T(8,128)(2,1)}, u32[]{:S(2)}, u32[]{:S(2)}) async-start(bf16[4,768,512]{1,2,0:T(8,128)(2,1)} %bitcast.78), calls=%async_computation | async-start | bytes 6291456 | tf_op jit(solution)/shard_map/all_to_all | solution.py:35
  165.4 11.4 %all_gather.23 = bf16[768,512]{1,0:T(8,128)(2,1)S(1)} all-gather(bf16[768,128]{1,0:T(8,128)(2,1)S(1)} %get-tuple-element.25), channel_id=1, replica_groups=mesh['pole'=4,'row'=2,'col'=4] {'pole'}, dimensions={1}, use_global_device_ids=true | all-gather | bytes 983040 | tf_op jit(solution)/shard_map/all_gather | solution.py:30
  176.9 12.1 %all_gather.22 = bf16[768,512]{1,0:T(8,128)(2,1)S(1)} all-gather(bf16[768,128]{1,0:T(8,128)(2,1)S(1)} %get-tuple-element.24), channel_id=1, replica_groups=mesh['pole'=4,'row'=2,'col'=4] {'pole'}, dimensions={1}, use_global_device_ids=true | all-gather | bytes 983040 | tf_op jit(solution)/shard_map/all_gather | solution.py:29
  189.0 2.3 fusion.37
  191.3 2.3 fusion.39
  193.5 1.6 add_convert_fusion
  195.2 1.6 subtract_convert_fusion.4
  196.8 2.7 convert_reduce_fusion
  202.6 33.3 %all-to-all-done = bf16[4,768,512]{1,2,0:T(8,128)(2,1)} async-done(((bf16[4,768,512]{1,2,0:T(8,128)(2,1)}), bf16[4,768,512]{1,2,0:T(8,128)(2,1)}, u32[]{:S(2)}, u32[]{:S(2)}) %all-to-all-start) | async-done | bytes 3145760 | tf_op jit(solution)/shard_map/all_to_all | solution.py:35
  235.8 2.6 convert_reduce_fusion.1
  241.7 1.3 copy.22
  243.0 29.8 %all_to_all.25 = bf16[8,128,512]{2,1,0:T(8,128)(2,1)S(1)} all-to-all(bf16[8,128,512]{2,1,0:T(8,128)(2,1)} %bitcast.81), channel_id=1, replica_groups=mesh['pole'=4,'row'=2,'col'=4] {'row','col'}, dimensions={0} | all-to-all | bytes 2097152 | tf_op jit(solution)/shard_map/all_to_all | solution.py:35
  273.0 7.3 %collective-permute-done.1 = bf16[128,512]{1,0:T(8,128)(2,1)S(1)} collective-permute-done((bf16[128,512]{1,0:T(8,128)(2,1)S(1)}, bf16[128,512]{1,0:T(8,128)(2,1)S(1)}, u32[]{:S(2)}, u32[]{:S(2)}) %collective-permute-start.1) | collective-permute-done | bytes 131104 | tf_op jit(solution)/shard_map/ppermute | solution.py:15
  280.4 3.6 %collective-permute-start.5 = (bf16[128,512]{1,0:T(8,128)(2,1)S(1)}, bf16[128,512]{1,0:T(8,128)(2,1)S(1)}, u32[]{:S(2)}, u32[]{:S(2)}) collective-permute-start(bf16[128,512]{1,0:T(8,128)(2,1)S(1)} %convert_reduce_fusion.2), channel_id=1, source_target_pairs={{0,7},{1,0},{2,1},{3,2},{4,3},{5,4},{6,5},{7,6},{8,15},{9,8},{10,9... | collective-permute-start | bytes 393224 | tf_op jit(solution)/shard_map/ppermute | solution.py:17
  283.9 3.8 %collective-permute-done.2 = bf16[128,512]{1,0:T(8,128)(2,1)S(1)} collective-permute-done((bf16[128,512]{1,0:T(8,128)(2,1)S(1)}, bf16[128,512]{1,0:T(8,128)(2,1)S(1)}, u32[]{:S(2)}, u32[]{:S(2)}) %collective-permute-start.2) | collective-permute-done | bytes 131104 | tf_op jit(solution)/shard_map/ppermute | solution.py:15
  288.7 3.2 collective-permute-start.6
  291.9 3.2 collective-permute-done.3
  295.1 4.5 %fusion.28 = f32[768,1,512]{0,2,1:T(8,128)} fusion(f32[768,2,256]{0,2,1:T(8,128)} %bitcast.74, f32[768,2,256]{0,2,1:T(8,128)} %bitcast.72, f32[]{:T(128)} %bitcast.18, f32[]{:T(128)} %bitcast.17), kind=kLoop, calls=%fused_computation.41 | loop fusion | flops 1966080 | bytes 4718600 | tf_op jit(solution)/shard_map/sub | solution.py:103
  299.6 3.1 copy.23
  302.6 4.3 %all-to-all-start.3 = ((f32[4,768,128]{2,1,0:T(8,128)}), f32[4,768,128]{2,1,0:T(8,128)}, u32[]{:S(2)}, u32[]{:S(2)}) async-start(f32[4,768,128]{2,1,0:T(8,128)} %copy.23), calls=%async_computation.3 | async-start | bytes 3145728 | tf_op jit(solution)/shard_map/all_to_all | solution.py:35
  307.0 3.6 %collective-permute-start.7 = (bf16[128,512]{1,0:T(8,128)(2,1)S(1)}, bf16[128,512]{1,0:T(8,128)(2,1)S(1)}, u32[]{:S(2)}, u32[]{:S(2)}) collective-permute-start(bf16[128,512]{1,0:T(8,128)(2,1)S(1)} %collective-permute-done.6), channel_id=1, source_target_pairs={{0,7},{1,0},{2,1},{3,2},{4,3},{5,4},{6,5},{7,6},{8,15},{9,8},{10,9... | collective-permute-start | bytes 393224 | tf_op jit(solution)/shard_map/ppermute | solution.py:17
  310.7 3.6 %collective-permute-done.7 = bf16[128,512]{1,0:T(8,128)(2,1)S(1)} collective-permute-done((bf16[128,512]{1,0:T(8,128)(2,1)S(1)}, bf16[128,512]{1,0:T(8,128)(2,1)S(1)}, u32[]{:S(2)}, u32[]{:S(2)}) %collective-permute-start.7) | collective-permute-done | bytes 131104 | tf_op jit(solution)/shard_map/ppermute | solution.py:17
  316.1 2.5 fusion.43
  318.6 8.9 %all-to-all-done.3 = f32[4,768,128]{2,1,0:T(8,128)} async-done(((f32[4,768,128]{2,1,0:T(8,128)}), f32[4,768,128]{2,1,0:T(8,128)}, u32[]{:S(2)}, u32[]{:S(2)}) %all-to-all-start.3) | async-done | bytes 1572896 | tf_op jit(solution)/shard_map/all_to_all | solution.py:35
  327.5 3.5 all-to-all-start.4
  331.0 3.7 %fusion.19 = f32[1,768,2,512]{1,3,2,0:T(8,128)} fusion(f32[768,2,256]{0,2,1:T(8,128)} %bitcast.73, f32[768,2,256]{0,2,1:T(8,128)} %bitcast.75), kind=kLoop, calls=%fused_computation.22 | loop fusion | flops 786432 | bytes 6291456 | tf_op jit(solution)/shard_map/broadcast_in_dim | solution.py:108
  334.7 5.7 %copy.24 = f32[1,768,2,512]{3,2,1,0:T(2,128)} copy(f32[1,768,2,512]{1,3,2,0:T(8,128)} %fusion.19) | data formatting | bytes 6291456
  340.4 2.3 reduce_sum.48
  342.7 3.4 sub.71
  (69 shorter events, 15.4 us)
Async XLA Ops:
  7.2 17.4 %copy-start = (f32[1,2,512,512]{3,2,1,0:T(8,128)S(1)}, f32[1,2,512,512]{3,2,1,0:T(8,128)}, u32[]{:S(2)}) copy-start(f32[1,2,512,512]{3,2,1,0:T(8,128)} %param.10) | copy-start | bytes 6291460
  7.2 58.3 %all-gather.5.cloned.1.call-start = ((), (), s32[]{:S(2)}) async-start(), calls=%async_computation.6 | async-start | bytes 2359296 | tf_op jit(solution)/shard_map/all_gather | solution.py:73
  9.3 2.7 collective-permute-start
  65.5 1.9 copy-start.6
  84.6 76.2 %all-to-all-start.1 = ((bf16[4,768,512]{1,2,0:T(8,128)(2,1)}), bf16[4,768,512]{1,2,0:T(8,128)(2,1)}, u32[]{:S(2)}, u32[]{:S(2)}) async-start(bf16[4,768,512]{1,2,0:T(8,128)(2,1)} %bitcast.79), calls=%async_computation.1 | async-start | bytes 6291456 | tf_op jit(solution)/shard_map/all_to_all | solution.py:35
  89.4 14.2 %all-gather.3.cloned.1.call-start = ((), (), s32[]{:S(2)}) async-start(), calls=%async_computation.5 | async-start | bytes 2359296 | tf_op jit(solution)/shard_map/all_gather | solution.py:73
  103.7 1.9 copy-start.7
  160.8 75.1 %all-to-all-start = ((bf16[4,768,512]{1,2,0:T(8,128)(2,1)}), bf16[4,768,512]{1,2,0:T(8,128)(2,1)}, u32[]{:S(2)}, u32[]{:S(2)}) async-start(bf16[4,768,512]{1,2,0:T(8,128)(2,1)} %bitcast.78), calls=%async_computation | async-start | bytes 6291456 | tf_op jit(solution)/shard_map/all_to_all | solution.py:35
  196.8 3.7 %copy-start.3 = (bf16[768,512]{0,1:T(8,128)(2,1)}, bf16[768,512]{0,1:T(8,128)(2,1)S(1)}, u32[]{:S(2)}) copy-start(bf16[768,512]{0,1:T(8,128)(2,1)S(1)} %subtract_convert_fusion.4) | copy-start | bytes 2359300
  199.5 1.1 copy-start.1
  235.8 2.6 copy-start.4
  238.4 1.2 copy-start.2
  240.6 1.0 copy-start.8
  243.0 44.8 %copy-start.9 = (f32[1,2]{1,0:T(1,128)S(1)}, f32[1,2]{1,0:T(1,128)}, u32[]{:S(2)}) copy-start(f32[1,2]{1,0:T(1,128)} %param.9) | copy-start | bytes 28
  273.0 7.4 %collective-permute-start.1 = (bf16[128,512]{1,0:T(8,128)(2,1)S(1)}, bf16[128,512]{1,0:T(8,128)(2,1)S(1)}, u32[]{:S(2)}, u32[]{:S(2)}) collective-permute-start(bf16[128,512]{1,0:T(8,128)(2,1)S(1)} %convert_reduce_fusion.2), channel_id=1, source_target_pairs={{0,1},{1,2},{2,3},{3,4},{4,5},{5,6},{6,7},{7,0},{8,9},{9,10},{10,1... | collective-permute-start | bytes 393224 | tf_op jit(solution)/shard_map/ppermute | solution.py:15
  280.4 7.4 %collective-permute-start.2 = (bf16[128,512]{1,0:T(8,128)(2,1)S(1)}, bf16[128,512]{1,0:T(8,128)(2,1)S(1)}, u32[]{:S(2)}, u32[]{:S(2)}) collective-permute-start(bf16[128,512]{1,0:T(8,128)(2,1)S(1)} %collective-permute-done.1), channel_id=1, source_target_pairs={{0,1},{1,2},{2,3},{3,4},{4,5},{5,6},{6,7},{7,0},{8,9},{9,10},{10,1... | collective-permute-start | bytes 393224 | tf_op jit(solution)/shard_map/ppermute | solution.py:15
  280.4 8.3 %collective-permute-start.5 = (bf16[128,512]{1,0:T(8,128)(2,1)S(1)}, bf16[128,512]{1,0:T(8,128)(2,1)S(1)}, u32[]{:S(2)}, u32[]{:S(2)}) collective-permute-start(bf16[128,512]{1,0:T(8,128)(2,1)S(1)} %convert_reduce_fusion.2), channel_id=1, source_target_pairs={{0,7},{1,0},{2,1},{3,2},{4,3},{5,4},{6,5},{7,6},{8,15},{9,8},{10,9... | collective-permute-start | bytes 393224 | tf_op jit(solution)/shard_map/ppermute | solution.py:17
  287.8 7.3 %collective-permute-start.3 = (bf16[128,512]{1,0:T(8,128)(2,1)S(1)}, bf16[128,512]{1,0:T(8,128)(2,1)S(1)}, u32[]{:S(2)}, u32[]{:S(2)}) collective-permute-start(bf16[128,512]{1,0:T(8,128)(2,1)S(1)} %collective-permute-done.2), channel_id=1, source_target_pairs={{0,1},{1,2},{2,3},{3,4},{4,5},{5,6},{6,7},{7,0},{8,9},{9,10},{10,1... | collective-permute-start | bytes 393224 | tf_op jit(solution)/shard_map/ppermute | solution.py:15
  288.7 18.3 %collective-permute-start.6 = (bf16[128,512]{1,0:T(8,128)(2,1)S(1)}, bf16[128,512]{1,0:T(8,128)(2,1)S(1)}, u32[]{:S(2)}, u32[]{:S(2)}) collective-permute-start(bf16[128,512]{1,0:T(8,128)(2,1)S(1)} %collective-permute-done.5), channel_id=1, source_target_pairs={{0,7},{1,0},{2,1},{3,2},{4,3},{5,4},{6,5},{7,6},{8,15},{9,8},{10,9... | collective-permute-start | bytes 393224 | tf_op jit(solution)/shard_map/ppermute | solution.py:17
  295.1 15.5 %collective-permute-start.4 = (bf16[128,512]{1,0:T(8,128)(2,1)S(1)}, bf16[128,512]{1,0:T(8,128)(2,1)S(1)}, u32[]{:S(2)}, u32[]{:S(2)}) collective-permute-start(bf16[128,512]{1,0:T(8,128)(2,1)S(1)} %collective-permute-done.3), channel_id=1, source_target_pairs={{0,1},{1,2},{2,3},{3,4},{4,5},{5,6},{6,7},{7,0},{8,9},{9,10},{10,1... | collective-permute-start | bytes 393224 | tf_op jit(solution)/shard_map/ppermute | solution.py:15
  302.6 24.8 %all-to-all-start.3 = ((f32[4,768,128]{2,1,0:T(8,128)}), f32[4,768,128]{2,1,0:T(8,128)}, u32[]{:S(2)}, u32[]{:S(2)}) async-start(f32[4,768,128]{2,1,0:T(8,128)} %copy.23), calls=%async_computation.3 | async-start | bytes 3145728 | tf_op jit(solution)/shard_map/all_to_all | solution.py:35
  307.0 7.3 %collective-permute-start.7 = (bf16[128,512]{1,0:T(8,128)(2,1)S(1)}, bf16[128,512]{1,0:T(8,128)(2,1)S(1)}, u32[]{:S(2)}, u32[]{:S(2)}) collective-permute-start(bf16[128,512]{1,0:T(8,128)(2,1)S(1)} %collective-permute-done.6), channel_id=1, source_target_pairs={{0,7},{1,0},{2,1},{3,2},{4,3},{5,4},{6,5},{7,6},{8,15},{9,8},{10,9... | collective-permute-start | bytes 393224 | tf_op jit(solution)/shard_map/ppermute | solution.py:17
  314.8 1.3 copy-start.5
  327.5 18.6 %all-to-all-start.4 = ((f32[4,128,512]{2,1,0:T(8,128)}), f32[4,128,512]{2,1,0:T(8,128)S(1)}, u32[]{:S(2)}, u32[]{:S(2)}) async-start(f32[4,128,512]{2,1,0:T(8,128)} %bitcast.23), calls=%async_computation.4 | async-start | bytes 2097152 | tf_op jit(solution)/shard_map/all_to_all | solution.py:35
Sparse Core Ops, SparseCore 0:
  45.8 19.6 all-gather.4
  92.4 11.2 all-gather.2
